TPU v7x, 32 devices: a whole 2x2x4 slice. The times are simulated.
32 devices in a mesh: phi: 8 (over z, core), mom: 4 (over y, x).
Axes of the slice: x: 2, y: 2, z: 4, core: 2. Of those that a mesh axis runs over, the one named last changes fastest.
Arguments:
- spectra: float32 [32, 4, 16, 64, 256], P('mom', None, 'phi'), may hold values from 0.1 to 3
- production: bfloat16 [32, 32], replicated, may hold values from 0 to 0.119628906
- bin_group: int32 [32], replicated, may hold values from 0 to 3
- parent_of: int32 [4], replicated, may hold values from 0 to 3
- diffusivity: float32 [64, 256], replicated, may hold values from 0.05 to 0.22
- height_inverse: float32 [64, 64], replicated, may hold values from -1 to 1, as said below
- loss_rate: float32 [32], P('mom'), may hold values from 2 to 20
- density: float32 [16, 64, 256], P('phi'), may hold values from 0.5 to 2
Outputs:
- spectra_out: float32 [32, 4, 16, 64, 256], P('mom', None, 'phi')
Inputs may be any that keep to these rules, and one draw needn't show every extreme that they name: `height_inverse`: diagonal entries lie between 0.7 and 1, off-diagonal entries are small.
All inputs are finite; a program needn't handle non-finite values.
Results may differ from a plain program's by a relative error of at most 0.00085.
Values may be sent and summed in bfloat16 or wider, within the bound.
A program may use at most 64 MiB of HBM per device.

v0:
```python
import jax
import jax.numpy as jnp
from jax import lax
from jax.sharding import PartitionSpec as P


def padded_2(cells, sides, width):
    for axis, dim in sides:
        count = lax.axis_size(axis)
        head = lax.slice_in_dim(cells, 0, width, axis=dim)
        tail = lax.slice_in_dim(cells, cells.shape[dim] - width, cells.shape[dim], axis=dim)
        cells = jnp.concatenate(
            [
                lax.ppermute(tail, axis, [(i, (i + 1) % count) for i in range(count)]),
                cells,
                lax.ppermute(head, axis, [((i + 1) % count, i) for i in range(count)]),
            ],
            axis=dim,
        )
    return cells


def passed_along(block, axis, distance):
    devices = range(lax.axis_size(axis))
    route = [(i - distance, i) for i in devices if i - distance in devices]
    return lax.ppermute(block, axis, route)


def one_step(
    state, production, bin_group, parent_of, diffusivity, height_inverse, loss_rate, density
):
    bins_here = state.shape[0]
    species = state.shape[1]
    onehot = (parent_of[:, None] == jnp.arange(species, dtype=jnp.int32)[None, :]).astype(
        jnp.float32
    )
    parents = jnp.einsum("st,qtxzr->qsxzr", onehot, state, precision=lax.Precision.HIGHEST).astype(
        jnp.bfloat16
    )
    same = bin_group[:, None] == bin_group[None, :]
    kernel = jnp.where(same, production, jnp.zeros_like(production))
    first_bin = lax.axis_index("mom") * bins_here
    flat_parents = parents.reshape(bins_here, -1)
    kernel_rows = lax.dynamic_slice_in_dim(kernel, first_bin, bins_here, 0)
    source = jnp.dot(
        kernel_rows,
        lax.all_gather(flat_parents, "mom", axis=0, tiled=True),
        preferred_element_type=jnp.float32,
    )
    sourced = state + source.reshape(state.shape)
    padded = padded_2(sourced.astype(jnp.bfloat16), (("phi", 2),), 1).astype(sourced.dtype)
    lap_phi = padded[:, :, 2:] + padded[:, :, :-2] - 2.0 * sourced
    pad_r = jnp.pad(sourced, ((0, 0), (0, 0), (0, 0), (0, 0), (1, 1)))
    lap_r = pad_r[..., 2:] + pad_r[..., :-2] - 2.0 * sourced
    moved = sourced + diffusivity * lap_phi + 0.5 * diffusivity * lap_r
    pad_z = jnp.pad(moved, ((0, 0), (0, 0), (0, 0), (1, 1), (0, 0)))
    halfway = moved + 0.25 * (pad_z[:, :, :, 2:] + pad_z[:, :, :, :-2] - 2.0 * moved)
    settled = jnp.einsum(
        "yz,psxzr->psxyr", height_inverse, halfway, precision=lax.Precision.HIGHEST
    )
    loss_coef = loss_rate[:, None, None, None, None] * density[None, None]
    upper_settled, upper_rate = passed_along((settled[:1], loss_rate[:1]), "mom", -1)
    upper_coef = upper_rate[:, None, None, None, None] * density[None, None]
    coef_next = jnp.concatenate([loss_coef[1:], upper_coef], axis=0)
    settled_next = jnp.concatenate([settled[1:], upper_settled], axis=0)
    right_side = (1.0 - 0.5 * loss_coef) * settled + 0.5 * coef_next * settled_next
    denominator = 1.0 + 0.5 * loss_coef
    offsets = right_side / denominator
    factors = 0.5 * coef_next / denominator
    local_c = jnp.zeros(state.shape[1:], jnp.float32)
    local_g = jnp.ones(factors.shape[1:], jnp.float32)
    for level in range(bins_here - 1, -1, -1):
        local_c = offsets[level] + factors[level] * local_c
        local_g = factors[level] * local_g

    def relay_step(index, incoming):
        return passed_along(local_c + local_g * incoming, "mom", -1)

    incoming = lax.fori_loop(0, lax.axis_size("mom") - 1, relay_step, jnp.zeros_like(local_c))
    current = incoming
    levels = []
    for level in range(bins_here - 1, -1, -1):
        current = offsets[level] + factors[level] * current
        levels.append(current)
    return jnp.stack(levels[::-1], axis=0)


def local(
    spectra, production, bin_group, parent_of, diffusivity, height_inverse, loss_rate, density
):
    state = spectra
    state = one_step(
        state, production, bin_group, parent_of, diffusivity, height_inverse, loss_rate, density
    )
    return state


def solution(mesh):
    return jax.shard_map(
        local,
        mesh=mesh,
        in_specs=(
            P("mom", None, "phi", None, None),
            P(),
            P(),
            P(),
            P(),
            P(),
            P("mom"),
            P("phi", None, None),
        ),
        out_specs=P("mom", None, "phi", None, None),
        check_vma=False,
    )
```

profile of v0, /device:TPU:0, one launch (start us, length us, event | category | flops | bytes accessed | tf_op | source)
XLA Modules:
  0.0 232.6 jit_solution(12985421989858237578)
XLA Ops:
  6.5 0.0 copy-start
  6.5 0.0 all-gather.2.cloned.1.call-start
  6.5 8.7 %convert_bitcast_fusion = bf16[8,4,2,64,256]{4,1,3,2,0:T(4,128)(2,1)S(1)} fusion(f32[8,4,2,64,256]{4,3,2,1,0:T(8,128)} %param.10, s32[4]{0:T(128)} %param.13), kind=kOutput, calls=%fused_computation.29 | convolution fusion | flops 51380240 | bytes 6291472 | tf_op jit(solution)/shard_map/st,qtxzr->qsxzr/dot_general | solution.py:37
  15.3 0.4 copy.12
  15.7 0.0 copy-start.7
  15.7 0.0 copy-start.8
  15.7 0.0 copy-start.4
  15.7 2.5 %copy.16 = bf16[1,8,512,256]{3,1,2,0:T(8,128)(2,1)} copy(bf16[1,8,512,256]{3,2,1,0:T(8,128)(2,1)S(1)} %bitcast.138) | data formatting | bytes 4194304
  18.2 0.0 all-gather.2.cloned.1.call-update
  18.2 0.0 copy-done.7
  18.2 1.3 collective-permute-start.3
  19.6 0.0 copy-done.8
  19.6 0.1 dynamic-slice
  19.6 0.0 copy-done.4
  19.6 0.2 broadcast_multiply_fusion
  19.8 88.9 %all-gather.2.cloned.1.call-done = bf16[32,131072]{1,0:T(8,128)(2,1)} async-done(((bf16[8,131072]{1,0:T(8,128)(2,1)}), bf16[32,131072]{1,0:T(8,128)(2,1)}) %all-gather.2.cloned.1.call-update) | async-done | bytes 8388624 | tf_op jit(solution)/shard_map/all_gather | solution.py:47
  108.7 0.0 copy-start.3
  108.7 4.8 %fusion.29 = f32[8,131072]{1,0:T(8,128)S(1)} fusion(bf16[32,131072]{1,0:T(8,128)(2,1)} %all-gather.2.cloned.1.call-done, bf16[32,32]{1,0:T(8,128)(2,1)} %param.11, s32[]{:T(128)S(6)} %select_n.8, s32[32]{0:T(128)S(1)} %copy-done.8, s32[8]{0:T(128)S(1)} %dynamic-slice), kind=kOutput, calls=%fused_computation.76 | convolution fusion | flops 67109376 | bytes 12585124 | tf_op jit(solution)/shard_map/dot_general | solution.py:45
  113.5 0.0 copy-done.3
  113.5 1.6 fusion.42
  115.2 0.0 copy-start.5
  115.2 0.2 fusion.43
  115.4 0.2 collective-permute-start.1
  115.7 3.5 %collective-permute-start.2 = (bf16[8,4,1,64,256]{4,3,2,1,0:T(8,128)(2,1)S(1)}, bf16[8,4,1,64,256]{4,3,2,1,0:T(8,128)(2,1)S(1)}, u32[]{:S(2)}, u32[]{:S(2)}) collective-permute-start(bf16[8,4,1,64,256]{4,3,2,1,0:T(8,128)(2,1)S(1)} %get-tuple-element.43), channel_id=1, source_target_pairs={{4,0},{8,4},{12,8},{16,12},{20,16},{24,20},{28,24},{0,28},{5,1},{9... | collective-permute-start | bytes 3145736 | tf_op jit(solution)/shard_map/ppermute | solution.py:16
  119.2 0.0 copy-done.5
  119.2 0.2 fusion.44
  119.4 0.3 fusion.27
  119.7 0.0 collective-permute-done.3
  119.7 0.6 multiply_bitcast_fusion.1
  120.4 0.3 fusion.25
  120.7 20.4 %collective-permute-done.1 = bf16[8,4,1,64,256]{4,3,2,1,0:T(8,128)(2,1)S(1)} collective-permute-done((bf16[8,4,1,64,256]{4,3,2,1,0:T(8,128)(2,1)S(1)}, bf16[8,4,1,64,256]{4,3,2,1,0:T(8,128)(2,1)S(1)}, u32[]{:S(2)}, u32[]{:S(2)}) %collective-permute-start.1) | collective-permute-done | bytes 1048608 | tf_op jit(solution)/shard_map/ppermute | solution.py:14
  141.0 0.0 collective-permute-done.2
  141.0 0.6 maximum_convert_fusion
  141.7 2.9 %fusion.9 = f32[8,4,2,64,256]{4,3,2,1,0:T(8,128)S(1)} fusion(f32[8,4,2,64,256]{4,3,2,1,0:T(8,128)S(1)} %get-tuple-element.41, f32[8,4,4,64,256]{4,3,2,1,0:T(8,128)S(1)} %maximum_convert_fusion, f32[64,256]{1,0:T(8,128)S(1)} %broadcast_multiply_fusion.2, f32[64,256]{1,0:T(8,128)S(1)} %copy-done.5), kind=kLoop, calls=%fused_computation.13 | loop fusion | flops 9437184 | bytes 16908288 | tf_op jit(solution)/shard_map/add | solution.py:55
  144.5 0.0 copy-done
  144.6 5.4 %fusion.18 = f32[8,4,2,64,256]{4,3,2,1,0:T(8,128)S(1)} fusion(f32[8,4,2,64,256]{4,3,2,1,0:T(8,128)S(1)} %fusion.9, f32[64,64]{1,0:T(8,128)S(1)} %copy-done), kind=kOutput, calls=%fused_computation.26 | convolution fusion | flops 810549248 | bytes 8404992 | tf_op jit(solution)/shard_map/yz,psxzr->psxyr/dot_general | solution.py:58
  150.0 1.3 collective-permute-start.4
  151.3 0.1 maximum_multiply_fusion.1
  151.4 0.1 slice_bitcast_fusion.8
  151.5 0.4 slice.141
  152.0 14.0 %collective-permute-done.4 = f32[1,4,2,64,256]{4,3,2,1,0:T(8,128)S(1)} collective-permute-done((f32[1,4,2,64,256]{4,3,2,1,0:T(8,128)S(1)}, f32[1,4,2,64,256]{4,3,2,1,0:T(8,128)S(1)}, u32[]{:S(2)}, u32[]{:S(2)}) %collective-permute-start.4) | collective-permute-done | bytes 524320 | tf_op jit(solution)/shard_map/ppermute | solution.py:26
  166.0 1.6 fusion.14
  167.6 0.0 copy-start.1
  167.7 2.0 copy-done.1
  169.7 0.4 multiply_add_fusion.8
  170.1 48.9 %while.10 = (s32[]{:T(128)}, f32[4,2,64,256]{3,2,1,0:T(8,128)S(1)}, f32[1,2,64,256]{3,2,1,0:T(8,128)S(1)}, f32[4,2,64,256]{3,2,1,0:T(8,128)S(1)}, s32[]{:T(128)}) while((s32[]{:T(128)}, f32[4,2,64,256]{3,2,1,0:T(8,128)S(1)}, f32[1,2,64,256]{3,2,1,0:T(8,128)S(1)}, f32[4,2,64,256]{3,2,1,0:T(8,128)S(1)}, s32[]{:T(128)}) %tuple.34), condition=%wide.region_1.2_spmd, body=%wide.region_0.1_spmd.sunk | while | flops 262146 | bytes 3801189 | solution.py:79
  170.1 0.1 multiply_add_fusion.13
  170.2 1.3 collective-permute-start
  171.5 15.6 %collective-permute-done = f32[4,2,64,256]{3,2,1,0:T(8,128)S(1)} collective-permute-done((f32[4,2,64,256]{3,2,1,0:T(8,128)S(1)}, f32[4,2,64,256]{3,2,1,0:T(8,128)S(1)}, u32[]{:S(2)}, u32[]{:S(2)}) %collective-permute-start) | collective-permute-done | bytes 524320 | tf_op jit(solution)/shard_map/while/body/eval_jaxpr/ppermute | solution.py:26
  187.1 0.1 multiply_add_fusion.13
  187.2 1.3 collective-permute-start
  188.5 15.0 %collective-permute-done = f32[4,2,64,256]{3,2,1,0:T(8,128)S(1)} collective-permute-done((f32[4,2,64,256]{3,2,1,0:T(8,128)S(1)}, f32[4,2,64,256]{3,2,1,0:T(8,128)S(1)}, u32[]{:S(2)}, u32[]{:S(2)}) %collective-permute-start) | collective-permute-done | bytes 524320 | tf_op jit(solution)/shard_map/while/body/eval_jaxpr/ppermute | solution.py:26
  203.5 0.1 multiply_add_fusion.13
  203.6 1.3 collective-permute-start
  204.9 14.1 %collective-permute-done = f32[4,2,64,256]{3,2,1,0:T(8,128)S(1)} collective-permute-done((f32[4,2,64,256]{3,2,1,0:T(8,128)S(1)}, f32[4,2,64,256]{3,2,1,0:T(8,128)S(1)}, u32[]{:S(2)}, u32[]{:S(2)}) %collective-permute-start) | collective-permute-done | bytes 524320 | tf_op jit(solution)/shard_map/while/body/eval_jaxpr/ppermute | solution.py:26
  219.0 0.0 copy-start.2
  219.0 2.8 %bitcast_dynamic-update-slice_fusion.7 = (f32[8,4,2,64,256]{4,3,2,1,0:T(8,128)S(1)}, f32[4,2,64,256]{3,2,1,0:T(8,128)S(1)}, f32[4,2,64,256]{3,2,1,0:T(8,128)S(1)}, f32[4,2,64,256]{3,2,1,0:T(8,128)S(1)}) fusion(f32[8,4,2,64,256]{4,3,2,1,0:T(8,128)} %copy-done.1, f32[2,64,256]{2,1,0:T(8,128)S(1)} %get-tuple-element.52, ...), kind=kLoop, calls=%fused_computation.51 | loop fusion | flops 2097151 | bytes 7864320
  221.8 0.7 copy-done.2
  222.5 0.1 bitcast_dynamic-update-slice_fusion.6
  222.6 0.1 bitcast_dynamic-update-slice_fusion.4
  222.7 0.1 bitcast_dynamic-update-slice_fusion.2
  222.9 0.0 copy-start.6
  222.9 2.0 copy-done.6
  224.9 0.9 bitcast_dynamic-update-slice_fusion
  (7 shorter events, 0.2 us)
Async XLA Ops:
  6.5 138.0 %copy-start = (f32[64,64]{1,0:T(8,128)S(1)}, f32[64,64]{1,0:T(8,128)}, u32[]{:S(2)}) copy-start(f32[64,64]{1,0:T(8,128)} %param.15) | copy-start | bytes 49156
  6.5 102.2 %all-gather.2.cloned.1.call-start = ((), (), s32[]{:S(2)}) async-start(), calls=%async_computation | async-start | bytes 10485760 | tf_op jit(solution)/shard_map/all_gather | solution.py:47
  15.7 2.6 %copy-start.7 = (f32[8]{0:T(128)S(1)}, f32[8]{0:T(128)}, u32[]{:S(2)}) copy-start(f32[8]{0:T(128)} %param.16) | copy-start | bytes 100
  15.7 3.9 %copy-start.8 = (s32[32]{0:T(128)S(1)}, s32[32]{0:T(128)}, u32[]{:S(2)}) copy-start(s32[32]{0:T(128)} %param.12) | copy-start | bytes 388
  15.7 4.0 %copy-start.4 = (f32[2,64,256]{2,1,0:T(8,128)S(1)}, f32[2,64,256]{2,1,0:T(8,128)}, u32[]{:S(2)}) copy-start(f32[2,64,256]{2,1,0:T(8,128)} %param.17) | copy-start | bytes 393220
  18.2 101.5 %collective-permute-start.3 = (f32[1]{0:T(128)S(1)}, f32[1]{0:T(128)}, u32[]{:S(2)}, u32[]{:S(2)}) collective-permute-start(f32[1]{0:T(128)S(1)} %bitcast.140), channel_id=1, source_target_pairs={{1,0},{2,1},{3,2},{5,4},{6,5},{7,6},{9,8},{10,9},{11,10},{13,12},{... | collective-permute-start | bytes 20 | tf_op jit(solution)/shard_map/ppermute | solution.py:26
  108.7 4.8 %copy-start.3 = (f32[8,4,2,64,256]{4,3,2,1,0:T(8,128)S(1)}, f32[8,4,2,64,256]{4,3,2,1,0:T(8,128)}, u32[]{:S(2)}) copy-start(f32[8,4,2,64,256]{4,3,2,1,0:T(8,128)} %param.10) | copy-start | bytes 12582916
  115.2 4.0 %copy-start.5 = (f32[64,256]{1,0:T(8,128)S(1)}, f32[64,256]{1,0:T(8,128)}, u32[]{:S(2)}) copy-start(f32[64,256]{1,0:T(8,128)} %param.14) | copy-start | bytes 196612
  115.4 25.6 %collective-permute-start.1 = (bf16[8,4,1,64,256]{4,3,2,1,0:T(8,128)(2,1)S(1)}, bf16[8,4,1,64,256]{4,3,2,1,0:T(8,128)(2,1)S(1)}, u32[]{:S(2)}, u32[]{:S(2)}) collective-permute-start(bf16[8,4,1,64,256]{4,3,2,1,0:T(8,128)(2,1)S(1)} %get-tuple-element.42), channel_id=1, source_target_pairs={{0,4},{4,8},{8,12},{12,16},{16,20},{20,24},{24,28},{28,0},{1,5},{5... | collective-permute-start | bytes 3145736 | tf_op jit(solution)/shard_map/ppermute | solution.py:14
  115.7 25.4 %collective-permute-start.2 = (bf16[8,4,1,64,256]{4,3,2,1,0:T(8,128)(2,1)S(1)}, bf16[8,4,1,64,256]{4,3,2,1,0:T(8,128)(2,1)S(1)}, u32[]{:S(2)}, u32[]{:S(2)}) collective-permute-start(bf16[8,4,1,64,256]{4,3,2,1,0:T(8,128)(2,1)S(1)} %get-tuple-element.43), channel_id=1, source_target_pairs={{4,0},{8,4},{12,8},{16,12},{20,16},{24,20},{28,24},{0,28},{5,1},{9... | collective-permute-start | bytes 3145736 | tf_op jit(solution)/shard_map/ppermute | solution.py:16
  150.0 16.0 %collective-permute-start.4 = (f32[1,4,2,64,256]{4,3,2,1,0:T(8,128)S(1)}, f32[1,4,2,64,256]{4,3,2,1,0:T(8,128)S(1)}, u32[]{:S(2)}, u32[]{:S(2)}) collective-permute-start(f32[1,4,2,64,256]{4,3,2,1,0:T(8,128)S(1)} %slice.142), channel_id=1, source_target_pairs={{1,0},{2,1},{3,2},{5,4},{6,5},{7,6},{9,8},{10,9},{11,10},{13,12},{... | collective-permute-start | bytes 1572872 | tf_op jit(solution)/shard_map/ppermute | solution.py:26
  167.6 2.0 copy-start.1
  170.2 16.9 %collective-permute-start = (f32[4,2,64,256]{3,2,1,0:T(8,128)S(1)}, f32[4,2,64,256]{3,2,1,0:T(8,128)S(1)}, u32[]{:S(2)}, u32[]{:S(2)}) collective-permute-start(f32[4,2,64,256]{3,2,1,0:T(8,128)S(1)} %multiply_add_fusion.13), channel_id=1, source_target_pairs={{1,0},{2,1},{3,2},{5,4},{6,5},{7,6},{9,8},{10,9},{11,10},{13,12},{... | collective-permute-start | bytes 1572872 | tf_op jit(solution)/shard_map/while/body/eval_jaxpr/ppermute | solution.py:26
  187.2 16.3 %collective-permute-start = (f32[4,2,64,256]{3,2,1,0:T(8,128)S(1)}, f32[4,2,64,256]{3,2,1,0:T(8,128)S(1)}, u32[]{:S(2)}, u32[]{:S(2)}) collective-permute-start(f32[4,2,64,256]{3,2,1,0:T(8,128)S(1)} %multiply_add_fusion.13), channel_id=1, source_target_pairs={{1,0},{2,1},{3,2},{5,4},{6,5},{7,6},{9,8},{10,9},{11,10},{13,12},{... | collective-permute-start | bytes 1572872 | tf_op jit(solution)/shard_map/while/body/eval_jaxpr/ppermute | solution.py:26
  203.6 15.4 %collective-permute-start = (f32[4,2,64,256]{3,2,1,0:T(8,128)S(1)}, f32[4,2,64,256]{3,2,1,0:T(8,128)S(1)}, u32[]{:S(2)}, u32[]{:S(2)}) collective-permute-start(f32[4,2,64,256]{3,2,1,0:T(8,128)S(1)} %multiply_add_fusion.13), channel_id=1, source_target_pairs={{1,0},{2,1},{3,2},{5,4},{6,5},{7,6},{9,8},{10,9},{11,10},{13,12},{... | collective-permute-start | bytes 1572872 | tf_op jit(solution)/shard_map/while/body/eval_jaxpr/ppermute | solution.py:26
  219.0 3.4 %copy-start.2 = (f32[8,4,2,64,256]{4,3,2,1,0:T(8,128)S(1)}, f32[8,4,2,64,256]{4,3,2,1,0:T(8,128)}, u32[]{:S(2)}) copy-start(f32[8,4,2,64,256]{4,3,2,1,0:T(8,128)} %copy-done.1) | copy-start | bytes 12582916
  222.9 2.0 copy-start.6
Sparse Core Ops, SparseCore 0:
  18.4 90.2 all-gather.1
where the time goes:
time: 233 us
  waiting for transfers between devices  168 us (72%)
  matrix products  18.9 us (8%)
  between operations  13.7 us (6%)
  other arithmetic  12.9 us (6%)
  starting transfers between devices  10.2 us (4%)
  local copies, waits for them, and re-layouts  8.76 us (4%)
    all_gather x1, waiting for transfers between devices, one_step(): lax.all_gather(flat_parents, 'mom', axis=0, tiled=True)  88.9 us
    ppermute x5, waiting for transfers between devices, passed_along(): return lax.ppermute(block, axis, route)  58.8 us
    ppermute x1, waiting for transfers between devices, padded_2(): lax.ppermute(tail, axis, [(i, (i + 1) % count) for i in range(count)])  20.4 us
    dot_general x1, matrix products, one_step(): jnp.einsum('st,qtxzr->qsxzr', onehot, state, precision=lax.Precision.HIGH...  8.71 us
    unnamed x22, local copies, waits for them, and re-layouts  7.36 us
    ppermute x5, starting transfers between devices, passed_along(): return lax.ppermute(block, axis, route)  6.46 us
    dot_general x1, matrix products, one_step(): jnp.einsum('yz,psxzr->psxyr', height_inverse, halfway, precision=lax.Prec...  5.41 us
    dot_general x1, matrix products, one_step(): jnp.dot(kernel_rows, lax.all_gather(flat_parents, 'mom', axis=0, tiled=Tr...  4.81 us
  transfers between devices with their start and end apart: 8, of which 6 were waited for; matrix products, arithmetic and copies ran while one was open for 4% of the time, Pallas kernels for 0%

commit v1 on v0

v1 whole, which is shorter than its diff:
```python
import functools
import math

import jax
import jax.numpy as jnp
from jax import lax
from jax.experimental import pallas as pl
from jax.experimental.pallas import tpu as pltpu
from jax.sharding import PartitionSpec as P

MESH = pl.DeviceIdType.MESH
ROWS = 16


def grid_of(count):
    columns = max(d for d in range(1, math.isqrt(count) + 1) if count % d == 0)
    return count // columns, columns


def dot(a, b):
    return jnp.dot(a, b, preferred_element_type=jnp.float32)


def dot_nt(a, b):
    return lax.dot_general(a, b, (((1,), (1,)), ((), ())), preferred_element_type=jnp.float32)


def onehot_bins(first_bins, bins, total):
    local = lax.broadcasted_iota(jnp.int32, (bins, ROWS, total), 0)
    whole = lax.broadcasted_iota(jnp.int32, (bins, ROWS, total), 2)
    parts = [
        jnp.where(local + first == whole, 1.0, 0.0).reshape(bins * ROWS, total)
        for first in first_bins
    ]
    return jnp.concatenate(parts, axis=0).astype(jnp.bfloat16)


def step_kernel(
    ny,
    nx,
    f_ref,
    kernel_ref,
    parent_ref,
    diff_ref,
    inverse_ref,
    rate_ref,
    density_ref,
    out_ref,
    comb,
    ysend,
    yrecv,
    acc,
    faces_out,
    faces_in,
    hin,
    hout,
    weight,
    wide,
    height,
    coef,
    x_send,
    x_recv,
    y_send,
    y_recv,
    f_send,
    f_recv,
    h_send,
    h_recv,
):
    bins, species, cells, heights, radii = f_ref.shape
    total_bins = kernel_ref.shape[0]
    count = ny * nx
    chunks = species * cells
    phi = lax.axis_index("phi")
    mom = lax.axis_index("mom")
    phis = lax.axis_size("phi")
    row, col = mom // nx, mom % nx
    right, left = (phi + 1) % phis, (phi + phis - 1) % phis

    barrier = pltpu.get_barrier_semaphore()
    for d in range(1, count):
        pl.semaphore_signal(
            barrier, inc=1, device_id={"mom": (mom + d) % count}, device_id_type=MESH
        )
    for side in (left, right):
        pl.semaphore_signal(barrier, inc=1, device_id={"phi": side}, device_id_type=MESH)

    def x_copy(c, d):
        return pltpu.make_async_remote_copy(
            src_ref=comb.at[c, 0],
            dst_ref=comb.at[c, d],
            send_sem=x_send.at[c, d - 1],
            recv_sem=x_recv.at[c, d - 1],
            device_id={"mom": row * nx + (col + d) % nx},
            device_id_type=MESH,
        )

    def y_copy(c, e):
        return pltpu.make_async_remote_copy(
            src_ref=ysend.at[c, e - 1],
            dst_ref=yrecv.at[c, e - 1],
            send_sem=y_send.at[c, e - 1],
            recv_sem=y_recv.at[c, e - 1],
            device_id={"mom": ((row + e) % ny) * nx + col},
            device_id_type=MESH,
        )

    def face_copy(s, side):
        return pltpu.make_async_remote_copy(
            src_ref=faces_out.at[s, side],
            dst_ref=faces_in.at[s, side],
            send_sem=f_send.at[s, side],
            recv_sem=f_recv.at[s, side],
            device_id={"phi": left if side == 0 else right},
            device_id_type=MESH,
        )

    def h_copy(s):
        return pltpu.make_async_remote_copy(
            src_ref=hout.at[s],
            dst_ref=hin.at[s],
            send_sem=h_send.at[s],
            recv_sem=h_recv.at[s],
            device_id={"mom": (mom + count - 1) % count},
            device_id_type=MESH,
        )

    def fill_parents(s):
        parent = parent_ref[s]
        for x in range(cells):
            for q in range(bins):
                comb[s * cells + x, 0, q] = f_ref[q, parent, x].astype(jnp.bfloat16)

    def send_parents(s):
        for x in range(cells):
            for d in range(1, nx):
                x_copy(s * cells + x, d).start()

    fill_parents(0)
    pl.semaphore_wait(barrier, count + 1)
    send_parents(0)

    @pl.loop(1, species)
    def _(s):
        fill_parents(s)
        send_parents(s)

    rows_1h = onehot_bins([(((row + e) % ny) * nx + col) * bins for e in range(ny)], bins, total_bins)
    cols_1h = onehot_bins(
        [(row * nx + (col + nx - d) % nx) * bins for d in range(nx)], bins, total_bins
    )
    mixed = dot_nt(dot(rows_1h, kernel_ref[...]).astype(jnp.bfloat16), cols_1h)
    r_at = lax.broadcasted_iota(jnp.int32, mixed.shape, 0) & (ROWS - 1)
    c_at = lax.broadcasted_iota(jnp.int32, mixed.shape, 1) & (ROWS - 1)
    wide[...] = jnp.where(r_at == c_at, mixed, 0.0).astype(jnp.bfloat16)

    group = height.shape[1] // heights
    a_at = lax.broadcasted_iota(jnp.int32, (heights, heights), 0)
    b_at = lax.broadcasted_iota(jnp.int32, (heights, heights), 1)
    stencil = jnp.where(a_at == b_at, 0.5, 0.0) + jnp.where(jnp.abs(a_at - b_at) == 1, 0.25, 0.0)
    both = jnp.dot(
        inverse_ref[...],
        stencil,
        precision=lax.Precision.HIGHEST,
        preferred_element_type=jnp.float32,
    )
    high = both.astype(jnp.bfloat16).astype(jnp.float32)
    tall_a = lax.broadcasted_iota(jnp.int32, (group, heights, heights), 1)
    tall_b = lax.broadcasted_iota(jnp.int32, (group, heights, heights), 2)
    spread = jnp.where(tall_a == tall_b, 1.0, 0.0).reshape(group * heights, heights)
    spread = spread.astype(jnp.bfloat16)
    row_g = lax.broadcasted_iota(jnp.int32, (group, heights, group * heights), 0)
    col_g = lax.broadcasted_iota(jnp.int32, (group, heights, group * heights), 2)
    first = row_g * heights
    inside = jnp.where((col_g >= first) & (col_g < first + heights), 1.0, 0.0)
    inside = inside.reshape(group * heights, group * heights)
    for k, part in enumerate((high, both - high)):
        tall = jnp.concatenate([part] * group, axis=0).astype(jnp.bfloat16)
        height[k] = (dot_nt(tall, spread) * inside).astype(jnp.bfloat16)

    diff = diff_ref[...]
    lane = lax.broadcasted_iota(jnp.int32, diff.shape, 1)
    coef[0] = 1.0 - 3.0 * diff
    coef[1] = jnp.where(lane == 0, 0.0, 0.5 * diff)
    coef[2] = jnp.where(lane == radii - 1, 0.0, 0.5 * diff)

    for p in range(bins):
        half_rate = 0.5 * rate_ref[p]
        for x in range(cells):
            weight[p, x] = 1.0 / (1.0 + half_rate * density_ref[x])

    @pl.when(mom == count - 1)
    def _():
        hin[...] = jnp.zeros_like(hin)

    def mix(s):
        for x in range(cells):
            c = s * cells + x
            for d in range(1, nx):
                x_copy(c, d).wait_recv()

            @pl.loop(0, heights // ROWS)
            def _(k):
                at = pl.ds(pl.multiple_of(k * ROWS, ROWS), ROWS)
                block = comb[c, :, :, at, :].reshape(nx * bins * ROWS, radii)
                sums = dot(wide[...], block).reshape(ny, bins, ROWS, radii)
                acc[c, :, at, :] = f_ref[:, s, x, at, :] + sums[0]
                for e in range(1, ny):
                    ysend[c, e - 1, :, at, :] = sums[e].astype(jnp.bfloat16)

            for e in range(1, ny):
                y_copy(c, e).start()

    def source(s):
        for x in range(cells):
            c = s * cells + x
            for e in range(1, ny):
                y_copy(c, e).wait_recv()

            @pl.loop(0, bins)
            def _(p):
                value = acc[c, p]
                for e in range(1, ny):
                    value = value + yrecv[c, e - 1, p].astype(jnp.float32)
                acc[c, p] = value
                rounded = value.astype(jnp.bfloat16)
                if x == 0:
                    faces_out[s, 0, p] = rounded
                if x == cells - 1:
                    faces_out[s, 1, p] = rounded

            if x == 0:
                face_copy(s, 0).start()
            if x == cells - 1:
                face_copy(s, 1).start()

    def diffuse(s):
        face_copy(s, 0).wait_recv()
        face_copy(s, 1).wait_recv()
        first = s * cells
        per = group // cells

        @pl.loop(0, bins // per)
        def _(k):
            planes = []
            for j in range(per):
                p = k * per + j
                own = [acc[first + x, p] for x in range(cells)]
                before = [faces_in[s, 1, p].astype(jnp.float32)] + own[:-1]
                after = own[1:] + [faces_in[s, 0, p].astype(jnp.float32)]
                for x in range(cells):
                    moved = coef[0] * own[x] + diff_ref[...] * (before[x] + after[x])
                    moved += coef[1] * pltpu.roll(own[x], 1, 1)
                    moved += coef[2] * pltpu.roll(own[x], radii - 1, 1)
                    planes.append(moved)
            moved = jnp.concatenate(planes, axis=0)
            high = moved.astype(jnp.bfloat16)
            low = (moved - high.astype(jnp.float32)).astype(jnp.bfloat16)
            settled = dot(height[0], high) + dot(height[0], low) + dot(height[1], high)
            for j in range(per):
                for x in range(cells):
                    n = j * cells + x
                    acc[first + x, k * per + j] = settled[n * heights : (n + 1) * heights]

    def solve(s):
        @pl.when(mom < count - 1)
        def _():
            h_copy(s).wait_recv()

        span = heights // 2
        for x in range(cells):
            @pl.loop(0, 2)
            def _(k):
                at = pl.ds(pl.multiple_of(k * span, span), span)
                carry = hin[s, x, at, :]
                for p in range(bins - 1, -1, -1):
                    settled = acc[s * cells + x, p, at, :]
                    total = 2.0 * settled + carry
                    both = total * weight[p, x, at, :]
                    out_ref[p, s, x, at, :] = both - settled
                    carry = total - both
                hout[s, x, at, :] = carry

        @pl.when(mom > 0)
        def _():
            h_copy(s).start()

    @pl.loop(0, species + 2 + count)
    def _(i):
        @pl.when(i < species)
        def _():
            mix(i)

        @pl.when((i >= 1) & (i < species + 1))
        def _():
            source(i - 1)

        @pl.when((i >= 2) & (i < species + 2))
        def _():
            diffuse(i - 2)

        s = i - 2 - (count - 1 - mom)

        @pl.when((s >= 0) & (s < species))
        def _():
            solve(s)

    @pl.loop(0, species)
    def _(s):
        for x in range(cells):
            for d in range(1, nx):
                x_copy(s * cells + x, d).wait_send()
            for e in range(1, ny):
                y_copy(s * cells + x, e).wait_send()
        face_copy(s, 0).wait_send()
        face_copy(s, 1).wait_send()

        @pl.when(mom > 0)
        def _():
            h_copy(s).wait_send()


def local(
    ny,
    nx,
    spectra,
    production,
    bin_group,
    parent_of,
    diffusivity,
    height_inverse,
    loss_rate,
    density,
):
    bins, species, cells, heights, radii = spectra.shape
    same = bin_group[:, None] == bin_group[None, :]
    kernel = jnp.where(same, production, jnp.zeros_like(production))
    chunks = species * cells
    block = (bins, heights, radii)
    group = cells * max(1, 256 // (heights * cells))
    dma = pltpu.SemaphoreType.DMA
    vmem = pl.BlockSpec(memory_space=pltpu.VMEM)
    smem = pl.BlockSpec(memory_space=pltpu.SMEM)
    return pl.pallas_call(
        functools.partial(step_kernel, ny, nx),
        out_shape=jax.ShapeDtypeStruct(spectra.shape, jnp.float32),
        in_specs=[vmem, vmem, smem, vmem, vmem, smem, vmem],
        out_specs=vmem,
        scratch_shapes=[
            pltpu.VMEM((chunks, nx) + block, jnp.bfloat16),
            pltpu.VMEM((chunks, max(ny - 1, 1)) + block, jnp.bfloat16),
            pltpu.VMEM((chunks, max(ny - 1, 1)) + block, jnp.bfloat16),
            pltpu.VMEM((chunks,) + block, jnp.float32),
            pltpu.VMEM((species, 2) + block, jnp.bfloat16),
            pltpu.VMEM((species, 2) + block, jnp.bfloat16),
            pltpu.VMEM((species, cells, heights, radii), jnp.float32),
            pltpu.VMEM((species, cells, heights, radii), jnp.float32),
            pltpu.VMEM((bins, cells, heights, radii), jnp.float32),
            pltpu.VMEM((ny * bins * ROWS, nx * bins * ROWS), jnp.bfloat16),
            pltpu.VMEM((2, group * heights, group * heights), jnp.bfloat16),
            pltpu.VMEM((3, heights, radii), jnp.float32),
            dma((chunks, max(nx - 1, 1))),
            dma((chunks, max(nx - 1, 1))),
            dma((chunks, max(ny - 1, 1))),
            dma((chunks, max(ny - 1, 1))),
            dma((species, 2)),
            dma((species, 2)),
            dma((species,)),
            dma((species,)),
        ],
        compiler_params=pltpu.CompilerParams(
            collective_id=0, has_side_effects=True, vmem_limit_bytes=56 * 1024 * 1024
        ),
    )(spectra, kernel, parent_of, diffusivity, height_inverse, loss_rate, density)


def solution(mesh):
    ny, nx = grid_of(mesh.shape["mom"])
    return jax.shard_map(
        functools.partial(local, ny, nx),
        mesh=mesh,
        in_specs=(
            P("mom", None, "phi", None, None),
            P(),
            P(),
            P(),
            P(),
            P(),
            P("mom"),
            P("phi", None, None),
        ),
        out_specs=P("mom", None, "phi", None, None),
        check_vma=False,
    )
```

time: 233 us -> 91.5 us (0.39)
  waiting for transfers between devices: 168 us -> 0 us
  Pallas kernels: 0 us -> 85.2 us
  matrix products: 18.9 us -> 0 us
  between operations: 13.7 us -> 0.01 us
  other arithmetic: 12.9 us -> 1.4 us
  starting transfers between devices: 10.2 us -> 0 us
  local copies, waits for them, and re-layouts: 8.76 us -> 4.7 us
    all_gather x1 -> x0, waiting for transfers between devices: 88.9 us -> none  [one_step(): lax.all_gather(flat_parents, 'mom', axis=0, tiled=True)]
    pallas_call x0 -> x1, Pallas kernels: none -> 85.2 us  [local(): pl.pallas_call(functools.partial(step_kernel, ny, nx), out_shape=jax.Shap...]
    ppermute x7 -> x0, waiting for transfers between devices: 79.2 us -> none  [the longest x5 58.8 us: passed_along(): return lax.ppermute(block, axis, route)]
    dot_general x3 -> x0, matrix products: 18.9 us -> none  [the longest x1 8.71 us: one_step(): jnp.einsum('st,qtxzr->qsxzr', onehot, state, precision=lax.Precision.HIGH...]
    ppermute x7 -> x0, starting transfers between devices: 10.2 us -> none  [the longest x5 6.46 us: passed_along(): return lax.ppermute(block, axis, route)]
    add x5 -> x0, other arithmetic: 3.51 us -> none  [the longest x1 2.88 us: one_step(): moved = sourced + diffusivity * lap_phi + 0.5 * diffusivity * lap_r]
    unnamed x4 -> x0, other arithmetic: 2.99 us -> none
    unnamed x22 -> x1, local copies, waits for them, and re-layouts: 7.36 us -> 4.7 us
  transfers between devices with their start and end apart: 8 -> 0, of which waited for: 6 -> 0; matrix products, arithmetic and copies ran while one was open for 4% -> 0% of each run, Pallas kernels for 0% -> 0%
where the time goes in v1:
time: 91.5 us; the launch traced here: 91.4 us
  Pallas kernels  85.2 us (93%)
  local copies, waits for them, and re-layouts  4.7 us (5%)
  other arithmetic  1.4 us (2%)
    pallas_call x1, Pallas kernels, local(): pl.pallas_call(functools.partial(step_kernel, ny, nx), out_shape=jax.Shap...  85.2 us
    unnamed x1, local copies, waits for them, and re-layouts  4.7 us

profile of v1, /device:TPU:0, one launch (start us, length us, event | category | flops | bytes accessed | tf_op | source)
XLA Modules:
  0.0 91.4 jit_solution(9115627777881054669)
XLA Ops:
  0.0 1.4 %compare_select_fusion.kernel_ref = bf16[32,32]{1,0:T(8,128)(2,1)} fusion(bf16[32,32]{1,0:T(8,128)(2,1)} %param.9, s32[32]{0:T(128)} %param.10), kind=kLoop, calls=%fused_computation | loop fusion | flops 2048 | bytes 4224 | tf_op jit(solution)/shard_map/jit(_where)/select_n | solution.py:337
  1.4 85.2 %shard_map.82 = f32[8,4,2,64,256]{4,3,2,1,0:T(8,128)} custom-call(f32[8,4,2,64,256]{4,3,2,1,0:T(8,128)} %f_ref.1, bf16[32,32]{1,0:T(8,128)(2,1)} %compare_select_fusion.kernel_ref, s32[4]{0:T(128)} %parent_ref.1, f32[64,256]{1,0:T(8,128)} %diff_ref.1, f32[64,64]{1,0:T(8,128)} %inverse_ref.1, f32[8]{0:T(128)} %rate_ref.1, f32[2,64,256]{2,1,0:T(8,128)} %density_ref.1), custom_call_target="tpu_custom_call" | custom-call | tf_op jit(solution)/shard_map/pallas_call | solution.py:344
  86.7 4.7 %copy.10 = f32[8,4,2,64,256]{4,3,2,1,0:T(8,128)} copy(f32[8,4,2,64,256]{4,3,2,1,0:T(8,128)} %shard_map.82) | data formatting | bytes 8388608

commit v2 on v1

--- a/solution.py
+++ b/solution.py
@@ -38,45 +38,60 @@
 def step_kernel(
     ny,
     nx,
-    f_ref,
+    f_hbm,
     kernel_ref,
     parent_ref,
     diff_ref,
     inverse_ref,
     rate_ref,
     density_ref,
-    out_ref,
+    settled_ref,
+    hin,
+    f_ref,
     comb,
-    ysend,
-    yrecv,
+    psend,
+    precv,
     acc,
     faces_out,
     faces_in,
-    hin,
+    below,
+    above,
     hout,
     weight,
-    wide,
+    keep,
+    rates_out,
+    rates_in,
+    wide_0,
+    wide_1,
     height,
     coef,
+    in_sem,
+    out_sem,
     x_send,
     x_recv,
     y_send,
     y_recv,
     f_send,
     f_recv,
+    a_send,
+    a_recv,
     h_send,
     h_recv,
+    r_send,
+    r_recv,
 ):
     bins, species, cells, heights, radii = f_ref.shape
     total_bins = kernel_ref.shape[0]
     count = ny * nx
-    chunks = species * cells
+    wides = (wide_0, wide_1)
     phi = lax.axis_index("phi")
     mom = lax.axis_index("mom")
     phis = lax.axis_size("phi")
     row, col = mom // nx, mom % nx
     right, left = (phi + 1) % phis, (phi + phis - 1) % phis
 
+    load = pltpu.make_async_copy(f_hbm, f_ref, in_sem)
+    load.start()
     barrier = pltpu.get_barrier_semaphore()
     for d in range(1, count):
         pl.semaphore_signal(
@@ -85,23 +100,34 @@
     for side in (left, right):
         pl.semaphore_signal(barrier, inc=1, device_id={"phi": side}, device_id_type=MESH)
 
-    def x_copy(c, d):
+    def along_row(d):
+        return {"mom": row * nx + (col + d) % nx}
+
+    def along_col(e):
+        return {"mom": ((row + e) % ny) * nx + col}
+
+    def sizes(x):
+        return (nx, ny) if x % 2 == 0 else (ny, nx)
+
+    def parent_copy(s, x, d):
+        c = s * cells + x
         return pltpu.make_async_remote_copy(
             src_ref=comb.at[c, 0],
             dst_ref=comb.at[c, d],
             send_sem=x_send.at[c, d - 1],
             recv_sem=x_recv.at[c, d - 1],
-            device_id={"mom": row * nx + (col + d) % nx},
+            device_id=along_row(d) if x % 2 == 0 else along_col(d),
             device_id_type=MESH,
         )
 
-    def y_copy(c, e):
+    def partial_copy(s, x, e):
+        c = s * cells + x
         return pltpu.make_async_remote_copy(
-            src_ref=ysend.at[c, e - 1],
-            dst_ref=yrecv.at[c, e - 1],
+            src_ref=psend.at[c, e - 1],
+            dst_ref=precv.at[c, e - 1],
             send_sem=y_send.at[c, e - 1],
             recv_sem=y_recv.at[c, e - 1],
-            device_id={"mom": ((row + e) % ny) * nx + col},
+            device_id=along_col(e) if x % 2 == 0 else along_row(e),
             device_id_type=MESH,
         )
 
@@ -115,16 +141,40 @@
             device_id_type=MESH,
         )
 
-    def h_copy(s):
+    def below_copy(s):
+        return pltpu.make_async_remote_copy(
+            src_ref=below.at[s],
+            dst_ref=above.at[s],
+            send_sem=a_send.at[s],
+            recv_sem=a_recv.at[s],
+            device_id={"mom": (mom + count - 1) % count},
+            device_id_type=MESH,
+        )
+
+    def h_copy(s, k):
         return pltpu.make_async_remote_copy(
             src_ref=hout.at[s],
             dst_ref=hin.at[s],
-            send_sem=h_send.at[s],
+            send_sem=h_send.at[s, k],
             recv_sem=h_recv.at[s],
+            device_id={"mom": (mom + count - 1 - k) % count},
+            device_id_type=MESH,
+        )
+
+    def rate_copy():
+        return pltpu.make_async_remote_copy(
+            src_ref=rates_out,
+            dst_ref=rates_in,
+            send_sem=r_send,
+            recv_sem=r_recv,
             device_id={"mom": (mom + count - 1) % count},
             device_id_type=MESH,
         )
 
+    def settled_copy(s):
+        part = pl.ds(s * cells, cells)
+        return pltpu.make_async_copy(acc.at[part], settled_ref.at[part], out_sem.at[s])
+
     def fill_parents(s):
         parent = parent_ref[s]
         for x in range(cells):
@@ -133,9 +183,14 @@
 
     def send_parents(s):
         for x in range(cells):
-            for d in range(1, nx):
-                x_copy(s * cells + x, d).start()
-
+            for d in range(1, sizes(x)[0]):
+                parent_copy(s, x, d).start()
+
+    odd = mom % 2 == 1
+    ahead = 2
+    for p in range(bins):
+        rates_out[p] = jnp.full((8, radii), rate_ref[p], jnp.float32)
+    load.wait()
     fill_parents(0)
     pl.semaphore_wait(barrier, count + 1)
     send_parents(0)
@@ -143,16 +198,26 @@
     @pl.loop(1, species)
     def _(s):
         fill_parents(s)
-        send_parents(s)
-
-    rows_1h = onehot_bins([(((row + e) % ny) * nx + col) * bins for e in range(ny)], bins, total_bins)
-    cols_1h = onehot_bins(
-        [(row * nx + (col + nx - d) % nx) * bins for d in range(nx)], bins, total_bins
-    )
-    mixed = dot_nt(dot(rows_1h, kernel_ref[...]).astype(jnp.bfloat16), cols_1h)
-    r_at = lax.broadcasted_iota(jnp.int32, mixed.shape, 0) & (ROWS - 1)
-    c_at = lax.broadcasted_iota(jnp.int32, mixed.shape, 1) & (ROWS - 1)
-    wide[...] = jnp.where(r_at == c_at, mixed, 0.0).astype(jnp.bfloat16)
+
+        @pl.when(s < ahead)
+        def _():
+            send_parents(s)
+
+    @pl.when(odd)
+    def _():
+        rate_copy().start()
+
+    row_starts = [(row * nx + (col + d) % nx) * bins for d in range(nx)]
+    col_starts = [(((row + e) % ny) * nx + col) * bins for e in range(ny)]
+    row_froms = [(row * nx + (col + nx - d) % nx) * bins for d in range(nx)]
+    col_froms = [(((row + ny - e) % ny) * nx + col) * bins for e in range(ny)]
+    for to, source_from, ref in ((col_starts, row_froms, wide_0), (row_starts, col_froms, wide_1)):
+        rows_1h = onehot_bins(to, bins, total_bins)
+        cols_1h = onehot_bins(source_from, bins, total_bins)
+        mixed = dot_nt(dot(rows_1h, kernel_ref[...]).astype(jnp.bfloat16), cols_1h)
+        r_at = lax.broadcasted_iota(jnp.int32, mixed.shape, 0) & (ROWS - 1)
+        c_at = lax.broadcasted_iota(jnp.int32, mixed.shape, 1) & (ROWS - 1)
+        ref[...] = jnp.where(r_at == c_at, mixed, 0.0).astype(jnp.bfloat16)
 
     group = height.shape[1] // heights
     a_at = lax.broadcasted_iota(jnp.int32, (heights, heights), 0)
@@ -184,44 +249,62 @@
     coef[1] = jnp.where(lane == 0, 0.0, 0.5 * diff)
     coef[2] = jnp.where(lane == radii - 1, 0.0, 0.5 * diff)
 
-    for p in range(bins):
-        half_rate = 0.5 * rate_ref[p]
-        for x in range(cells):
-            weight[p, x] = 1.0 / (1.0 + half_rate * density_ref[x])
-
-    @pl.when(mom == count - 1)
+    for x in range(cells):
+        kept = jnp.ones((heights, radii), jnp.float32)
+        for p in range(bins):
+            part = 1.0 / (1.0 + 0.5 * rate_ref[p] * density_ref[x])
+            weight[p, x] = part
+            kept = kept * (1.0 - part)
+        keep[0, x] = kept
+
+    def keep_above():
+        rate_copy().wait_recv()
+        for x in range(cells):
+            kept = jnp.ones((heights // 8, 8, radii), jnp.float32)
+            dens = density_ref[x].reshape(heights // 8, 8, radii)
+            for p in range(bins):
+                kept = kept * (1.0 - 1.0 / (1.0 + 0.5 * rates_in[p] * dens))
+            keep[1, x] = kept.reshape(heights, radii)
+
+    @pl.when(mom >= count - 2)
     def _():
         hin[...] = jnp.zeros_like(hin)
 
     def mix(s):
         for x in range(cells):
             c = s * cells + x
-            for d in range(1, nx):
-                x_copy(c, d).wait_recv()
+            n1, n2 = sizes(x)
+            for d in range(1, n1):
+                parent_copy(s, x, d).wait_recv()
 
             @pl.loop(0, heights // ROWS)
             def _(k):
                 at = pl.ds(pl.multiple_of(k * ROWS, ROWS), ROWS)
-                block = comb[c, :, :, at, :].reshape(nx * bins * ROWS, radii)
-                sums = dot(wide[...], block).reshape(ny, bins, ROWS, radii)
+                block = comb[c, :n1, :, at, :].reshape(n1 * bins * ROWS, radii)
+                sums = dot(wides[x % 2][...], block).reshape(n2, bins, ROWS, radii)
                 acc[c, :, at, :] = f_ref[:, s, x, at, :] + sums[0]
-                for e in range(1, ny):
-                    ysend[c, e - 1, :, at, :] = sums[e].astype(jnp.bfloat16)
-
-            for e in range(1, ny):
-                y_copy(c, e).start()
+                for e in range(1, n2):
+                    psend[c, e - 1, :, at, :] = sums[e].astype(jnp.bfloat16)
+
+            for e in range(1, n2):
+                partial_copy(s, x, e).start()
+
+        @pl.when(s + ahead < species)
+        def _():
+            send_parents(s + ahead)
 
     def source(s):
         for x in range(cells):
             c = s * cells + x
-            for e in range(1, ny):
-                y_copy(c, e).wait_recv()
+            n2 = sizes(x)[1]
+            for e in range(1, n2):
+                partial_copy(s, x, e).wait_recv()
 
             @pl.loop(0, bins)
             def _(p):
                 value = acc[c, p]
-                for e in range(1, ny):
-                    value = value + yrecv[c, e - 1, p].astype(jnp.float32)
+                for e in range(1, n2):
+                    value = value + precv[c, e - 1, p].astype(jnp.float32)
                 acc[c, p] = value
                 rounded = value.astype(jnp.bfloat16)
                 if x == 0:
@@ -262,30 +345,52 @@
                     n = j * cells + x
                     acc[first + x, k * per + j] = settled[n * heights : (n + 1) * heights]
 
-    def solve(s):
-        @pl.when(mom < count - 1)
-        def _():
-            h_copy(s).wait_recv()
-
+        settled_copy(s).start()
         span = heights // 2
         for x in range(cells):
             @pl.loop(0, 2)
             def _(k):
                 at = pl.ds(pl.multiple_of(k * span, span), span)
-                carry = hin[s, x, at, :]
+                carry = jnp.zeros((span, radii), jnp.float32)
                 for p in range(bins - 1, -1, -1):
-                    settled = acc[s * cells + x, p, at, :]
-                    total = 2.0 * settled + carry
-                    both = total * weight[p, x, at, :]
-                    out_ref[p, s, x, at, :] = both - settled
-                    carry = total - both
-                hout[s, x, at, :] = carry
-
-        @pl.when(mom > 0)
-        def _():
-            h_copy(s).start()
-
-    @pl.loop(0, species + 2 + count)
+                    total = 2.0 * acc[first + x, p, at, :] + carry
+                    carry = total - total * weight[p, x, at, :]
+                below[s, x, at, :] = carry
+
+        @pl.when(odd)
+        def _():
+            below_copy(s).start()
+
+    def relay(s):
+        @pl.when(odd & (mom < count - 1))
+        def _():
+            h_copy(s, 0).wait_recv()
+
+        @pl.when(mom % 2 == 0)
+        def _():
+            @pl.when(s == 0)
+            def _():
+                keep_above()
+
+            below_copy(s).wait_recv()
+
+            @pl.when(mom < count - 2)
+            def _():
+                h_copy(s, 1).wait_recv()
+
+            for x in range(cells):
+                entering = above[s, x] + keep[1, x] * hin[s, x]
+                hin[s, x] = entering
+                hout[s, x] = below[s, x] + keep[0, x] * entering
+
+            @pl.when(mom > 0)
+            def _():
+                h_copy(s, 0).start()
+                h_copy(s, 1).start()
+
+    lag = (count - 1 - mom) // 2
+
+    @pl.loop(0, species + 3 + count // 2)
     def _(i):
         @pl.when(i < species)
         def _():
@@ -299,25 +404,57 @@
         def _():
             diffuse(i - 2)
 
-        s = i - 2 - (count - 1 - mom)
+        s = i - 2 - lag
 
         @pl.when((s >= 0) & (s < species))
         def _():
-            solve(s)
+            relay(s)
+
+    @pl.when(odd)
+    def _():
+        rate_copy().wait_send()
 
     @pl.loop(0, species)
     def _(s):
-        for x in range(cells):
-            for d in range(1, nx):
-                x_copy(s * cells + x, d).wait_send()
-            for e in range(1, ny):
-                y_copy(s * cells + x, e).wait_send()
+        settled_copy(s).wait()
+        for x in range(cells):
+            for d in range(1, sizes(x)[0]):
+                parent_copy(s, x, d).wait_send()
+            for e in range(1, sizes(x)[1]):
+                partial_copy(s, x, e).wait_send()
         face_copy(s, 0).wait_send()
         face_copy(s, 1).wait_send()
 
-        @pl.when(mom > 0)
-        def _():
-            h_copy(s).wait_send()
+        @pl.when(odd)
+        def _():
+            below_copy(s).wait_send()
+
+        @pl.when((mom % 2 == 0) & (mom > 0))
+        def _():
+            h_copy(s, 0).wait_send()
+            h_copy(s, 1).wait_send()
+
+
+def solve_kernel(settled_ref, hin_ref, rate_ref, density_ref, out_ref, weight):
+    bins, heights, radii = weight.shape
+
+    @pl.when(pl.program_id(1) == 0)
+    def _():
+        for p in range(bins):
+            weight[p] = 1.0 / (1.0 + 0.5 * rate_ref[p] * density_ref[0])
+
+    span = heights // 2
+
+    @pl.loop(0, 2)
+    def _(k):
+        at = pl.ds(pl.multiple_of(k * span, span), span)
+        carry = hin_ref[0, 0, at, :]
+        for p in range(bins - 1, -1, -1):
+            settled = settled_ref[0, p, at, :]
+            total = 2.0 * settled + carry
+            both = total * weight[p, at, :]
+            out_ref[p, 0, 0, at, :] = both - settled
+            carry = total - both
 
 
 def local(
@@ -337,41 +474,74 @@
     kernel = jnp.where(same, production, jnp.zeros_like(production))
     chunks = species * cells
     block = (bins, heights, radii)
+    plane = (heights, radii)
+    most = max(nx, ny)
     group = cells * max(1, 256 // (heights * cells))
     dma = pltpu.SemaphoreType.DMA
     vmem = pl.BlockSpec(memory_space=pltpu.VMEM)
     smem = pl.BlockSpec(memory_space=pltpu.SMEM)
-    return pl.pallas_call(
+    hbm = pl.BlockSpec(memory_space=pl.ANY)
+    tall, broad = ny * bins * ROWS, nx * bins * ROWS
+    settled, entering = pl.pallas_call(
         functools.partial(step_kernel, ny, nx),
-        out_shape=jax.ShapeDtypeStruct(spectra.shape, jnp.float32),
-        in_specs=[vmem, vmem, smem, vmem, vmem, smem, vmem],
-        out_specs=vmem,
+        out_shape=[
+            jax.ShapeDtypeStruct((chunks,) + block, jnp.float32),
+            jax.ShapeDtypeStruct((species, cells) + plane, jnp.float32),
+        ],
+        in_specs=[hbm, vmem, smem, vmem, vmem, smem, vmem],
+        out_specs=[hbm, vmem],
         scratch_shapes=[
-            pltpu.VMEM((chunks, nx) + block, jnp.bfloat16),
-            pltpu.VMEM((chunks, max(ny - 1, 1)) + block, jnp.bfloat16),
-            pltpu.VMEM((chunks, max(ny - 1, 1)) + block, jnp.bfloat16),
+            pltpu.VMEM(spectra.shape, jnp.float32),
+            pltpu.VMEM((chunks, most) + block, jnp.bfloat16),
+            pltpu.VMEM((chunks, most - 1) + block, jnp.bfloat16),
+            pltpu.VMEM((chunks, most - 1) + block, jnp.bfloat16),
             pltpu.VMEM((chunks,) + block, jnp.float32),
             pltpu.VMEM((species, 2) + block, jnp.bfloat16),
             pltpu.VMEM((species, 2) + block, jnp.bfloat16),
-            pltpu.VMEM((species, cells, heights, radii), jnp.float32),
-            pltpu.VMEM((species, cells, heights, radii), jnp.float32),
-            pltpu.VMEM((bins, cells, heights, radii), jnp.float32),
-            pltpu.VMEM((ny * bins * ROWS, nx * bins * ROWS), jnp.bfloat16),
+            pltpu.VMEM((species, cells) + plane, jnp.float32),
+            pltpu.VMEM((species, cells) + plane, jnp.float32),
+            pltpu.VMEM((species, cells) + plane, jnp.float32),
+            pltpu.VMEM((bins, cells) + plane, jnp.float32),
+            pltpu.VMEM((2, cells) + plane, jnp.float32),
+            pltpu.VMEM((bins, 8, radii), jnp.float32),
+            pltpu.VMEM((bins, 8, radii), jnp.float32),
+            pltpu.VMEM((tall, broad), jnp.bfloat16),
+            pltpu.VMEM((broad, tall), jnp.bfloat16),
             pltpu.VMEM((2, group * heights, group * heights), jnp.bfloat16),
-            pltpu.VMEM((3, heights, radii), jnp.float32),
-            dma((chunks, max(nx - 1, 1))),
-            dma((chunks, max(nx - 1, 1))),
-            dma((chunks, max(ny - 1, 1))),
-            dma((chunks, max(ny - 1, 1))),
+            pltpu.VMEM((3,) + plane, jnp.float32),
+            dma,
+            dma((species,)),
+            dma((chunks, most - 1)),
+            dma((chunks, most - 1)),
+            dma((chunks, most - 1)),
+            dma((chunks, most - 1)),
             dma((species, 2)),
             dma((species, 2)),
             dma((species,)),
             dma((species,)),
+            dma((species, 2)),
+            dma((species,)),
+            dma,
+            dma,
         ],
         compiler_params=pltpu.CompilerParams(
             collective_id=0, has_side_effects=True, vmem_limit_bytes=56 * 1024 * 1024
         ),
     )(spectra, kernel, parent_of, diffusivity, height_inverse, loss_rate, density)
+    return pl.pallas_call(
+        solve_kernel,
+        grid=(cells, species),
+        out_shape=jax.ShapeDtypeStruct(spectra.shape, jnp.float32),
+        in_specs=[
+            pl.BlockSpec((1,) + block, lambda x, s: (s * cells + x, 0, 0, 0)),
+            pl.BlockSpec((1, 1) + plane, lambda x, s: (s, x, 0, 0)),
+            smem,
+            pl.BlockSpec((1,) + plane, lambda x, s: (x, 0, 0)),
+        ],
+        out_specs=pl.BlockSpec((bins, 1, 1) + plane, lambda x, s: (0, s, x, 0, 0)),
+        scratch_shapes=[pltpu.VMEM(block, jnp.float32)],
+        compiler_params=pltpu.CompilerParams(vmem_limit_bytes=60 * 1024 * 1024),
+    )(settled, entering, loss_rate, density)
 
 
 def solution(mesh):

time: 91.5 us -> 86.7 us (0.948)
  local copies, waits for them, and re-layouts: 4.7 us -> 0 us
    unnamed x1 -> x0, local copies, waits for them, and re-layouts: 4.7 us -> none
    pallas_call x1 -> x2, Pallas kernels: 85.2 us -> 84.9 us  [the longest x1 77.7 us: local(): pl.pallas_call(functools.partial(step_kernel, ny, nx), out_shape=[jax.Sha...]
where the time goes in v2:
time: 86.7 us; the launch traced here: 86.4 us
  Pallas kernels  84.9 us (98%)
  other arithmetic  1.4 us (2%)
    pallas_call x1, Pallas kernels, local(): pl.pallas_call(functools.partial(step_kernel, ny, nx), out_shape=[jax.Sha...  77.7 us
    pallas_call x1, Pallas kernels, local(): pl.pallas_call(solve_kernel, grid=(cells, species), out_shape=jax.ShapeDt...  7.21 us

profile of v2, /device:TPU:0, one launch (start us, length us, event | category | flops | bytes accessed | tf_op | source)
XLA Modules:
  0.0 86.4 jit_solution(13974055717720253997)
XLA Ops:
  0.0 1.4 %compare_select_fusion.kernel_ref = bf16[32,32]{1,0:T(8,128)(2,1)} fusion(bf16[32,32]{1,0:T(8,128)(2,1)} %param.9, s32[32]{0:T(128)} %param.10), kind=kLoop, calls=%fused_computation | loop fusion | flops 2048 | bytes 4224 | tf_op jit(solution)/shard_map/jit(_where)/select_n | solution.py:474
  1.4 77.7 %shard_map.82 = (f32[8,8,64,256]{3,2,1,0:T(8,128)}, f32[4,2,64,256]{3,2,1,0:T(8,128)}) custom-call(f32[8,4,2,64,256]{4,3,2,1,0:T(8,128)} %f_hbm.1, bf16[32,32]{1,0:T(8,128)(2,1)} %compare_select_fusion.kernel_ref, s32[4]{0:T(128)} %parent_ref.1, f32[64,256]{1,0:T(8,128)} %diff_ref.1, f32[64,64]{1,0:T(8,128)} %inverse_ref.1, f32[8]{0:T(128)} %rate_ref.3, ...), custom_call_target="tpu_custom_call" | custom-call | tf_op jit(solution)/shard_map/pallas_call | solution.py:485
  79.1 7.2 %shard_map.83 = f32[8,4,2,64,256]{4,3,2,1,0:T(8,128)} custom-call(f32[8,8,64,256]{3,2,1,0:T(8,128)} %get-tuple-element.7.settled_ref, f32[4,2,64,256]{3,2,1,0:T(8,128)} %get-tuple-element.8.hin_ref, f32[8]{0:T(128)} %rate_ref.3, f32[2,64,256]{2,1,0:T(8,128)} %density_ref.3), custom_call_target="tpu_custom_call" | custom-call | tf_op jit(solution)/shard_map/pallas_call | solution.py:531

commit v3 on v2

--- a/solution.py
+++ b/solution.py
@@ -40,14 +40,20 @@
     nx,
     f_hbm,
     kernel_ref,
+    parent_hbm,
+    diff_hbm,
+    inverse_hbm,
+    rate_hbm,
+    density_hbm,
+    settled_ref,
+    hin,
+    weight,
+    f_ref,
     parent_ref,
     diff_ref,
     inverse_ref,
     rate_ref,
     density_ref,
-    settled_ref,
-    hin,
-    f_ref,
     comb,
     psend,
     precv,
@@ -57,7 +63,6 @@
     below,
     above,
     hout,
-    weight,
     keep,
     rates_out,
     rates_in,
@@ -90,8 +95,18 @@
     row, col = mom // nx, mom % nx
     right, left = (phi + 1) % phis, (phi + phis - 1) % phis
 
-    load = pltpu.make_async_copy(f_hbm, f_ref, in_sem)
+    load = pltpu.make_async_copy(f_hbm, f_ref, in_sem.at[0])
+    small = [
+        pltpu.make_async_copy(parent_hbm, parent_ref, in_sem.at[1]),
+        pltpu.make_async_copy(rate_hbm, rate_ref, in_sem.at[2]),
+        pltpu.make_async_copy(diff_hbm, diff_ref, in_sem.at[3]),
+        pltpu.make_async_copy(inverse_hbm, inverse_ref, in_sem.at[4]),
+        pltpu.make_async_copy(density_hbm, density_ref, in_sem.at[5]),
+    ]
+    small[0].start()
     load.start()
+    for copy in small[1:]:
+        copy.start()
     barrier = pltpu.get_barrier_semaphore()
     for d in range(1, count):
         pl.semaphore_signal(
@@ -188,8 +203,7 @@
 
     odd = mom % 2 == 1
     ahead = 2
-    for p in range(bins):
-        rates_out[p] = jnp.full((8, radii), rate_ref[p], jnp.float32)
+    small[0].wait()
     load.wait()
     fill_parents(0)
     pl.semaphore_wait(barrier, count + 1)
@@ -202,6 +216,11 @@
         @pl.when(s < ahead)
         def _():
             send_parents(s)
+
+    for copy in small[1:]:
+        copy.wait()
+    for p in range(bins):
+        rates_out[p] = jnp.full((8, radii), rate_ref[p], jnp.float32)
 
     @pl.when(odd)
     def _():
@@ -357,10 +376,6 @@
                     carry = total - total * weight[p, x, at, :]
                 below[s, x, at, :] = carry
 
-        @pl.when(odd)
-        def _():
-            below_copy(s).start()
-
     def relay(s):
         @pl.when(odd & (mom < count - 1))
         def _():
@@ -389,8 +404,9 @@
                 h_copy(s, 1).start()
 
     lag = (count - 1 - mom) // 2
-
-    @pl.loop(0, species + 3 + count // 2)
+    hold = 3
+
+    @pl.loop(0, species + 3 + max(hold - 2, 0) + count // 2)
     def _(i):
         @pl.when(i < species)
         def _():
@@ -404,7 +420,12 @@
         def _():
             diffuse(i - 2)
 
-        s = i - 2 - lag
+        for s in range(species):
+            @pl.when(odd & (i == max(s + 2, hold)))
+            def _():
+                below_copy(s).start()
+
+        s = i - 2 - max(hold - 2, 0) - lag
 
         @pl.when((s >= 0) & (s < species))
         def _():
@@ -435,14 +456,8 @@
             h_copy(s, 1).wait_send()
 
 
-def solve_kernel(settled_ref, hin_ref, rate_ref, density_ref, out_ref, weight):
-    bins, heights, radii = weight.shape
-
-    @pl.when(pl.program_id(1) == 0)
-    def _():
-        for p in range(bins):
-            weight[p] = 1.0 / (1.0 + 0.5 * rate_ref[p] * density_ref[0])
-
+def solve_kernel(settled_ref, hin_ref, weight_ref, out_ref):
+    bins, _, heights, _ = weight_ref.shape
     span = heights // 2
 
     @pl.loop(0, 2)
@@ -452,7 +467,7 @@
         for p in range(bins - 1, -1, -1):
             settled = settled_ref[0, p, at, :]
             total = 2.0 * settled + carry
-            both = total * weight[p, at, :]
+            both = total * weight_ref[p, 0, at, :]
             out_ref[p, 0, 0, at, :] = both - settled
             carry = total - both
 
@@ -479,19 +494,26 @@
     group = cells * max(1, 256 // (heights * cells))
     dma = pltpu.SemaphoreType.DMA
     vmem = pl.BlockSpec(memory_space=pltpu.VMEM)
-    smem = pl.BlockSpec(memory_space=pltpu.SMEM)
-    hbm = pl.BlockSpec(memory_space=pl.ANY)
+    hbm = pl.BlockSpec(memory_space=pltpu.HBM)
+    free = pl.BlockSpec(memory_space=pl.ANY)
+    stay = functools.partial(pltpu.with_memory_space_constraint, memory_space=pltpu.HBM)
     tall, broad = ny * bins * ROWS, nx * bins * ROWS
-    settled, entering = pl.pallas_call(
+    settled, entering, weight = pl.pallas_call(
         functools.partial(step_kernel, ny, nx),
         out_shape=[
             jax.ShapeDtypeStruct((chunks,) + block, jnp.float32),
             jax.ShapeDtypeStruct((species, cells) + plane, jnp.float32),
+            jax.ShapeDtypeStruct((bins, cells) + plane, jnp.float32),
         ],
-        in_specs=[hbm, vmem, smem, vmem, vmem, smem, vmem],
-        out_specs=[hbm, vmem],
+        in_specs=[hbm, vmem, hbm, hbm, hbm, hbm, hbm],
+        out_specs=[free, vmem, vmem],
         scratch_shapes=[
             pltpu.VMEM(spectra.shape, jnp.float32),
+            pltpu.SMEM(parent_of.shape, jnp.int32),
+            pltpu.VMEM(plane, jnp.float32),
+            pltpu.VMEM(height_inverse.shape, jnp.float32),
+            pltpu.SMEM(loss_rate.shape, jnp.float32),
+            pltpu.VMEM(density.shape, jnp.float32),
             pltpu.VMEM((chunks, most) + block, jnp.bfloat16),
             pltpu.VMEM((chunks, most - 1) + block, jnp.bfloat16),
             pltpu.VMEM((chunks, most - 1) + block, jnp.bfloat16),
@@ -501,7 +523,6 @@
             pltpu.VMEM((species, cells) + plane, jnp.float32),
             pltpu.VMEM((species, cells) + plane, jnp.float32),
             pltpu.VMEM((species, cells) + plane, jnp.float32),
-            pltpu.VMEM((bins, cells) + plane, jnp.float32),
             pltpu.VMEM((2, cells) + plane, jnp.float32),
             pltpu.VMEM((bins, 8, radii), jnp.float32),
             pltpu.VMEM((bins, 8, radii), jnp.float32),
@@ -509,7 +530,7 @@
             pltpu.VMEM((broad, tall), jnp.bfloat16),
             pltpu.VMEM((2, group * heights, group * heights), jnp.bfloat16),
             pltpu.VMEM((3,) + plane, jnp.float32),
-            dma,
+            dma((6,)),
             dma((species,)),
             dma((chunks, most - 1)),
             dma((chunks, most - 1)),
@@ -525,9 +546,17 @@
             dma,
         ],
         compiler_params=pltpu.CompilerParams(
-            collective_id=0, has_side_effects=True, vmem_limit_bytes=56 * 1024 * 1024
+            collective_id=0, has_side_effects=True, vmem_limit_bytes=28 * 1024 * 1024
         ),
-    )(spectra, kernel, parent_of, diffusivity, height_inverse, loss_rate, density)
+    )(
+        stay(spectra),
+        kernel,
+        stay(parent_of),
+        stay(diffusivity),
+        stay(height_inverse),
+        stay(loss_rate),
+        stay(density),
+    )
     return pl.pallas_call(
         solve_kernel,
         grid=(cells, species),
@@ -535,13 +564,11 @@
         in_specs=[
             pl.BlockSpec((1,) + block, lambda x, s: (s * cells + x, 0, 0, 0)),
             pl.BlockSpec((1, 1) + plane, lambda x, s: (s, x, 0, 0)),
-            smem,
-            pl.BlockSpec((1,) + plane, lambda x, s: (x, 0, 0)),
+            pl.BlockSpec((bins, 1) + plane, lambda x, s: (0, x, 0, 0)),
         ],
         out_specs=pl.BlockSpec((bins, 1, 1) + plane, lambda x, s: (0, s, x, 0, 0)),
-        scratch_shapes=[pltpu.VMEM(block, jnp.float32)],
-        compiler_params=pltpu.CompilerParams(vmem_limit_bytes=60 * 1024 * 1024),
-    )(settled, entering, loss_rate, density)
+        compiler_params=pltpu.CompilerParams(vmem_limit_bytes=16 * 1024 * 1024),
+    )(settled, entering, weight)
 
 
 def solution(mesh):

time: 86.7 us -> 78.4 us (0.904); the launches traced: 86.4 us -> 77.2 us
  Pallas kernels: 84.9 us -> 76.4 us
    pallas_call x1, Pallas kernels: 77.7 us -> 72.5 us  [local(): pl.pallas_call(functools.partial(step_kernel, ny, nx), out_shape=[jax.Sha...]
    pallas_call x1, Pallas kernels: 7.21 us -> 3.88 us  [local(): pl.pallas_call(solve_kernel, grid=(cells, species), out_shape=jax.ShapeDt...]
where the time goes in v3:
time: 78.4 us; the launch traced here: 77.2 us
  Pallas kernels  76.4 us (97%)
  other arithmetic  0.8 us (1%)
    pallas_call x1, Pallas kernels, local(): pl.pallas_call(functools.partial(step_kernel, ny, nx), out_shape=[jax.Sha...  72.5 us
    pallas_call x1, Pallas kernels, local(): pl.pallas_call(solve_kernel, grid=(cells, species), out_shape=jax.ShapeDt...  3.88 us

profile of v3, /device:TPU:0, one launch (start us, length us, event | category | flops | bytes accessed | tf_op | source)
XLA Modules:
  0.0 77.2 jit_solution(5816536212041962650)
XLA Ops:
  0.0 0.8 %compare_select_fusion.kernel_ref = bf16[32,32]{1,0:T(8,128)(2,1)S(1)} fusion(bf16[32,32]{1,0:T(8,128)(2,1)} %param.9, s32[32]{0:T(128)} %param.10), kind=kLoop, calls=%fused_computation | loop fusion | flops 2048 | bytes 4224 | tf_op jit(solution)/shard_map/jit(_where)/select_n | solution.py:489
  0.8 72.5 %shard_map.82 = (f32[8,8,64,256]{3,2,1,0:T(8,128)S(1)}, f32[4,2,64,256]{3,2,1,0:T(8,128)S(1)}, f32[8,2,64,256]{3,2,1,0:T(8,128)S(1)}) custom-call(f32[8,4,2,64,256]{4,3,2,1,0:T(8,128)} %f_hbm.1, bf16[32,32]{1,0:T(8,128)(2,1)S(1)} %compare_select_fusion.kernel_ref, s32[4]{0:T(128)} %parent_hbm.1, f32[64,256]{1,0:T(8,128)} %diff_hbm.1, f32[64,64]{1,0:T(8,128)} %inverse_hbm.1, ...), custom_call_target="tpu_custom_call" | custom-call | tf_op jit(solution)/shard_map/pallas_call | solution.py:501
  73.3 3.9 %shard_map.83 = f32[8,4,2,64,256]{4,3,2,1,0:T(8,128)} custom-call(f32[8,8,64,256]{3,2,1,0:T(8,128)S(1)} %get-tuple-element.8.settled_ref, f32[4,2,64,256]{3,2,1,0:T(8,128)S(1)} %get-tuple-element.9.hin_ref, f32[8,2,64,256]{3,2,1,0:T(8,128)S(1)} %get-tuple-element.10.weight_ref), custom_call_target="tpu_custom_call" | custom-call | tf_op jit(solution)/shard_map/pallas_call | solution.py:560
